TPU v7x, 128 devices: a whole 4x4x4 slice. The times are simulated.
128 devices in a mesh: section: 8 (over y, x_hi), dp: 16 (over z, x_lo, core).
Axes of the slice: x: 4 (x_hi: 2, x_lo: 2; x = x_hi * 2 + x_lo), y: 4, z: 4, core: 2. Of those that a mesh axis runs over, the one named last changes fastest.
Arguments:
- saved: bfloat16 [8, 2048, 7168], P('section', 'dp')
- top_grad: bfloat16 [2048, 7168], P('dp')
- down_weight: bfloat16 [8, 256, 7168], P('section'), may hold values from -0.0625 to 0.0625
- up_weight: bfloat16 [8, 256, 7168], P('section'), may hold values from -0.1875 to 0.1875
Outputs:
- section_grads: bfloat16 [8, 2048, 7168], P('section', 'dp')
- updates: bfloat16 [8, 2, 256, 7168], P('section')
- grad_norms: float32 [8, 2], P('section')
All inputs are finite; a program needn't handle non-finite values.
Results may differ from a plain program's by a relative error of at most 0.0087.
Values may be sent and summed in bfloat16 or wider, within the bound.
A program may use at most 128 MiB of HBM per device.

v0:
```python
import functools
import math

import jax
import jax.numpy as jnp
from jax import lax
from jax.experimental import pallas as pl
from jax.experimental.pallas import tpu as pltpu
from jax.sharding import PartitionSpec as P

D = 7168
LAT = 256
ITERS = 5
TOK = 128
ROWS = 16
PAIRS = TOK // ROWS
CHUNKS = 4
WIDE = D // CHUNKS
SMALL = 8
SMALLS = TOK // SMALL
PACK = D // 2
PARTS = ((0, 1024), (1024, 1024), (2048, 1024), (3072, 512))
HALF = LAT // 2
BLOCKS = 8
BLOCK = D // BLOCKS
PEERS = 8
Z = 4
SPAN = D // Z
SECTIONS = 8

norm_eps = 1e-06
frob_eps = 1e-07
coef_a = 3.4445
coef_b = -4.775
coef_c = 2.0315

MESH = pl.DeviceIdType.MESH
f32 = jnp.float32
bf16 = jnp.bfloat16
HIGHEST = lax.Precision.HIGHEST


def remote(src, dst, send, recv, device):
    return pltpu.make_async_remote_copy(
        src_ref=src, dst_ref=dst, send_sem=send, recv_sem=recv, device_id=device, device_id_type=MESH
    )


def nt_dot(a, b, precision=None):
    return lax.dot_general(
        a, b, (((1,), (1,)), ((), ())), preferred_element_type=f32, precision=precision
    )


def tn_dot(a, b):
    return lax.dot_general(a, b, (((0,), (0,)), ((), ())), preferred_element_type=f32)


def split(a):
    high = a.astype(bf16)
    return high, (a - high.astype(f32)).astype(bf16)


def dot(a, b):
    return jnp.dot(a, b, preferred_element_type=f32)


def exact_dot(a, b):
    return jnp.dot(a, b, precision=HIGHEST, preferred_element_type=f32)


def three_dot(a, b):
    (a_high, a_low), (b_high, b_low) = split(a), split(b)
    return dot(a_high, b_high) + (dot(a_high, b_low) + dot(a_low, b_high))


def newton_schulz(gram):
    total = None
    eye = diagonal_mask().astype(f32)
    for step in range(ITERS):
        mul = exact_dot if step < 2 else three_dot
        poly = coef_a * eye + coef_b * gram + coef_c * mul(gram, gram)
        if step < ITERS - 1:
            gram = mul(mul(poly, gram), poly)
        total = poly if total is None else three_dot(poly, total)
    return total


def diagonal_mask():
    return lax.broadcasted_iota(jnp.int32, (LAT, LAT), 0) == lax.broadcasted_iota(
        jnp.int32, (LAT, LAT), 1
    )


def backward_kernel(
    saved, top, w_down, w_up, grads_out, gathered, poly_out, norm_out,
    x_v, x_p, wd_v, wu_v, wut_v, normed_v, og_v, og_p, ig_v, ig_p, inv_v, latent_v, slope_v, act_v, lat_v,
    big_all, small_all, give_v, take_v, own, poly_v, norm_v,
    load_sem, wd_sem, chain_send, chain_recv, big_send, big_recv, small_send, small_recv, store_sem,
    give_send, give_recv, ring_send, ring_recv, core_send, core_recv, poly_send, poly_recv,
):
    s = lax.axis_index("section")
    d = lax.axis_index("dp")
    core = lax.rem(d, 2)
    q = lax.div(d, 2)
    x = lax.rem(q, 2)
    z = lax.div(q, 2)
    up = lax.rem(z + 1, Z)
    down = lax.rem(z + 3, Z)
    far = lax.rem(z + 2, Z)
    is_top = s == SECTIONS - 1
    has_lower = s > 0

    def device(z_at, x_at, core_at):
        return (s, z_at * 4 + x_at * 2 + core_at)

    across = device(z, 1 - x, core)
    above = device(up, x, core)
    below = device(down, x, core)
    sibling = device(z, x, 1 - core)

    loads = [
        pltpu.make_async_copy(saved, x_v, load_sem.at[0]),
        pltpu.make_async_copy(w_up, wu_v, load_sem.at[1]),
    ]
    for k in range(BLOCKS):
        part = pl.ds((k % 2) * PACK + (k // 2) * BLOCK, BLOCK)
        loads.append(
            pltpu.make_async_copy(w_down.at[:, pl.ds(k * BLOCK, BLOCK)], wd_v.at[:, part], wd_sem.at[k])
        )
    for load in loads:
        load.start()
    top_load = pltpu.make_async_copy(top, og_v, load_sem.at[2])

    @pl.when(is_top)
    def _():
        top_load.start()

    barrier = pltpu.get_barrier_semaphore()
    pl.semaphore_signal(barrier, inc=1, device_id=sibling, device_id_type=MESH)
    pl.semaphore_signal(barrier, inc=1, device_id=across, device_id_type=MESH)
    for k in range(1, Z):
        for core_at in range(2):
            pl.semaphore_signal(
                barrier, inc=1, device_id=device(lax.rem(z + k, Z), x, core_at), device_id_type=MESH
            )

    @pl.when(jnp.logical_not(is_top))
    def _():
        pl.semaphore_signal(barrier, inc=1, device_id=(s + 1, d), device_id_type=MESH)

    def pack(flat, packed, i):
        rows = pl.ds(pl.multiple_of(i * ROWS, ROWS), ROWS)
        for k in range(Z):
            even = flat[rows, 2 * k * BLOCK:(2 * k + 1) * BLOCK].astype(f32)
            odd = flat[rows, (2 * k + 1) * BLOCK:(2 * k + 2) * BLOCK].astype(f32)
            cols = slice(k * BLOCK, (k + 1) * BLOCK)
            packed[2 * i, :, cols] = jnp.concatenate([even[:SMALL], odd[:SMALL]], axis=0).astype(bf16)
            packed[2 * i + 1, :, cols] = jnp.concatenate([even[SMALL:], odd[SMALL:]], axis=0).astype(bf16)

    def unpack(packed, flat, i):
        rows = pl.ds(pl.multiple_of(i * ROWS, ROWS), ROWS)
        for k in range(Z):
            cols = slice(k * BLOCK, (k + 1) * BLOCK)
            first = packed[2 * i, :, cols].astype(f32)
            second = packed[2 * i + 1, :, cols].astype(f32)
            even = jnp.concatenate([first[:SMALL], second[:SMALL]], axis=0)
            odd = jnp.concatenate([first[SMALL:], second[SMALL:]], axis=0)
            flat[rows, 2 * k * BLOCK:(2 * k + 1) * BLOCK] = even.astype(bf16)
            flat[rows, (2 * k + 1) * BLOCK:(2 * k + 2) * BLOCK] = odd.astype(bf16)

    loads[0].wait()

    def norm_rows(m, _):
        rows = pl.ds(pl.multiple_of(m * ROWS, ROWS), ROWS)
        total = jnp.zeros((ROWS, 1), f32)
        for j in range(CHUNKS):
            part = x_v[rows, j * WIDE:(j + 1) * WIDE].astype(f32)
            total += jnp.sum(part * part, axis=1, keepdims=True)
        inv = 1.0 / jnp.sqrt(total * (1.0 / D) + norm_eps)
        inv_v[rows, :] = jnp.broadcast_to(inv, (ROWS, 128))
        for j in range(CHUNKS):
            part = x_v[rows, j * WIDE:(j + 1) * WIDE].astype(f32)
            normed_v[rows, j * WIDE:(j + 1) * WIDE] = (part * inv).astype(bf16)
        pack(x_v, x_p, m)
        return 0

    lax.fori_loop(0, PAIRS, norm_rows, 0)
    loads[1].wait()

    def turn(k, _):
        for odd in range(2):
            cols = pl.ds(pl.multiple_of((2 * k + odd) * BLOCK, BLOCK), BLOCK)
            rows = pl.ds(pl.multiple_of(k * BLOCK, BLOCK), BLOCK)
            wut_v[rows, odd * LAT:(odd + 1) * LAT] = wu_v[:, cols].T
        return 0

    lax.fori_loop(0, Z, turn, 0)
    for load in loads[2:]:
        load.wait()

    def latent_part(k, acc):
        for odd in range(2):
            cols = pl.ds(pl.multiple_of((2 * k + odd) * BLOCK, BLOCK), BLOCK)
            part = pl.ds(pl.multiple_of(odd * PACK + k * BLOCK, BLOCK), BLOCK)
            acc = acc + nt_dot(normed_v[:, cols], wd_v[:, part])
        return acc

    latent = lax.fori_loop(0, Z, latent_part, jnp.zeros((TOK, LAT), f32))
    sigmoid = 1.0 / (1.0 + jnp.exp(-latent))
    latent_v[...] = latent
    act_v[...] = (latent * sigmoid).astype(bf16)
    slope_v[...] = sigmoid * (1.0 + latent * (1.0 - sigmoid))

    @pl.when(has_lower)
    def _():
        pl.semaphore_wait(barrier, PEERS + 1)

    @pl.when(jnp.logical_not(has_lower))
    def _():
        pl.semaphore_wait(barrier, PEERS)

    place = z * 2 + core

    def share(src_of, dst, send, recv, target_core, act):
        for k in range(Z):
            z_at = lax.rem(z + k, Z)
            copy = remote(src_of(z_at), dst, send, recv, device(z_at, x, target_core))
            if k:
                act(copy)
            else:
                @pl.when(core != target_core)
                def _():
                    act(copy)

    def share_own(src, dst, recv, target_core):
        @pl.when(core == target_core)
        def _():
            pltpu.make_async_copy(src, dst, recv).start()

    def span(z_at):
        return pl.ds(pl.multiple_of(z_at * SPAN, SPAN), SPAN)

    def share_normed(act):
        share(lambda z_at: normed_v.at[:, span(z_at)], big_all.at[place], big_send, big_recv.at[place], 0, act)
        share(lambda z_at: act_v, small_all.at[place], small_send, small_recv.at[place], 1, act)

    def start_normed():
        share_normed(lambda copy: copy.start())
        share_own(normed_v.at[:, span(z)], big_all.at[place], big_recv.at[place], 0)
        share_own(act_v, small_all.at[place], small_recv.at[place], 1)

    @pl.when(jnp.logical_not(is_top))
    def _():
        start_normed()

    @pl.when(is_top)
    def _():
        top_load.wait()

        def pack_top(i, _):
            pack(og_v, og_p, i)
            return 0

        lax.fori_loop(0, PAIRS, pack_top, 0)

    def chain_copy(m, j):
        cols = pl.ds(*PARTS[j])
        return remote(
            ig_p.at[m, :, cols], og_p.at[m, :, cols], chain_send.at[m, j], chain_recv.at[m, j],
            (jnp.maximum(s - 1, 0), d),
        )

    def share_grads(m, act):
        rows = pl.ds(pl.multiple_of(m * ROWS, ROWS), ROWS)
        share(
            lambda z_at: og_v.at[rows, span(z_at)], big_all.at[place, rows], big_send, big_recv.at[place], 1, act
        )
        share(lambda z_at: lat_v.at[rows], small_all.at[place, rows], small_send, small_recv.at[place], 0, act)

    def step(m):
        rows = pl.ds(pl.multiple_of(m * SMALL, SMALL), SMALL)
        acc = jnp.zeros((ROWS, 2 * LAT), f32)
        for j, (at, width) in enumerate(PARTS):

            @pl.when(jnp.logical_not(is_top))
            def _():
                chain_copy(m, j).wait_recv()

            acc += dot(og_p[m, :, at:at + width], wut_v[at:at + width, :])
        act_grad = acc[:SMALL, :LAT] + acc[SMALL:, LAT:]
        lat = (act_grad * slope_v[rows, :]).astype(bf16).astype(f32)
        inv = inv_v[rows, 0:1]
        mean = jnp.sum(lat * latent_v[rows, :], axis=1, keepdims=True) * (1.0 / D)
        pull = inv * inv * mean
        lat_twice = jnp.concatenate([lat, lat], axis=0).astype(bf16)
        inv_twice = jnp.concatenate([inv, inv], axis=0)
        pull_twice = jnp.concatenate([pull, pull], axis=0)
        for j, (at, width) in enumerate(PARTS):
            cols = slice(at, at + width)
            even = dot(lat_twice, wd_v[:, at:at + width])
            odd = dot(lat_twice, wd_v[:, PACK + at:PACK + at + width])
            ng = jnp.concatenate([even[:SMALL], odd[SMALL:]], axis=0)
            out = og_p[m, :, cols].astype(f32) + inv_twice * ng - pull_twice * x_p[m, :, cols].astype(f32)
            ig_p[m, :, cols] = out.astype(bf16)

            @pl.when(has_lower)
            def _():
                chain_copy(m, j).start()

        return lat

    def micro(i, _):
        rows = pl.ds(pl.multiple_of(i * ROWS, ROWS), ROWS)
        first = step(2 * i)
        second = step(2 * i + 1)
        lat_v[rows, :] = jnp.concatenate([first, second], axis=0).astype(bf16)

        @pl.when(jnp.logical_not(is_top))
        def _():
            unpack(og_p, og_v, i)

        share_grads(i, lambda copy: copy.start())
        share_own(og_v.at[rows, span(z)], big_all.at[place, rows], big_recv.at[place], 1)
        share_own(lat_v.at[rows], small_all.at[place, rows], small_recv.at[place], 0)
        unpack(ig_p, ig_v, i)
        return 0

    lax.fori_loop(0, PAIRS, micro, 0)

    @pl.when(is_top)
    def _():
        start_normed()

    store = pltpu.make_async_copy(ig_v, grads_out, store_sem.at[0])
    store.start()

    def arrived(p, _):
        pltpu.make_async_copy(big_all.at[p], big_all.at[p], big_recv.at[p]).wait()
        pltpu.make_async_copy(small_all.at[p], small_all.at[p], small_recv.at[p]).wait()
        return 0

    lax.fori_loop(0, PEERS, arrived, 0)

    left = small_all[...].reshape(PEERS * TOK, LAT).T

    def half_cols(x_at):
        return pl.ds(pl.multiple_of(x_at * BLOCK, BLOCK), BLOCK)

    def half_rows(half):
        return pl.ds(half * HALF, HALF)

    right = big_all[:, :, half_cols(1 - x)].reshape(PEERS * TOK, BLOCK)
    gives = []
    for half in range(2):
        give_v[half_rows(half)] = dot(left[half * HALF:(half + 1) * HALF], right).astype(bf16)
        copy = remote(
            give_v.at[half_rows(half)], take_v.at[half_rows(half)], give_send.at[half], give_recv.at[half], across
        )
        copy.start()
        gives.append(copy)
    mine = dot(left, big_all[:, :, half_cols(x)].reshape(PEERS * TOK, BLOCK))

    ring_copies = []
    core_copies = []

    def at(z_at, x_at, half):
        return own.at[z_at * 2 + x_at, half_rows(half)]

    def forward(z_at, x_at, half, to):
        copy = remote(
            at(z_at, x_at, half), at(z_at, x_at, half),
            ring_send.at[len(ring_copies)], ring_recv.at[z_at * 2 + x_at, half], to,
        )
        copy.start()
        ring_copies.append(copy)

    def to_sibling(z_at, x_at, half):
        copy = remote(
            at(z_at, x_at, half), gathered.at[core, z_at * 2 + x_at, half_rows(half)], core_send, core_recv, sibling
        )
        copy.start()
        core_copies.append(copy)

    def wait(z_at, x_at, half):
        part = at(z_at, x_at, half)
        pltpu.make_async_copy(part, part, ring_recv.at[z_at * 2 + x_at, half]).wait()

    def used(z_at, x_at):
        part = own[z_at * 2 + x_at]
        return nt_dot(part, part)

    for half in range(2):
        gives[half].wait_recv()
        total = mine[half * HALF:(half + 1) * HALF] + take_v[half_rows(half)].astype(f32)
        own[q, half_rows(half)] = total.astype(bf16)
        forward(z, x, half, above)
        forward(z, x, half, below)
        forward(z, x, half, across)
        to_sibling(z, x, half)
    gram = used(z, x)

    wait(down, x, 0)
    forward(down, x, 0, above)
    to_sibling(down, x, 0)
    wait(up, x, 0)
    to_sibling(up, x, 0)
    wait(z, 1 - x, 0)
    forward(z, 1 - x, 0, above)
    forward(z, 1 - x, 0, below)
    to_sibling(z, 1 - x, 0)
    wait(up, x, 1)
    forward(up, x, 1, below)
    to_sibling(up, x, 1)
    wait(down, x, 1)
    to_sibling(down, x, 1)
    wait(z, 1 - x, 1)
    forward(z, 1 - x, 1, above)
    forward(z, 1 - x, 1, below)
    to_sibling(z, 1 - x, 1)
    gram += used(down, x)
    gram += used(up, x)
    gram += used(z, 1 - x)
    for half in range(2):
        wait(far, x, half)
        forward(far, x, half, across)
        to_sibling(far, x, half)
    gram += used(far, x)
    for z_at in (up, down):
        for half in range(2):
            wait(z_at, 1 - x, half)
            to_sibling(z_at, 1 - x, half)
        gram += used(z_at, 1 - x)
    for half in range(2):
        wait(far, 1 - x, half)
        to_sibling(far, 1 - x, half)
    gram += used(far, 1 - x)
    store_own = pltpu.make_async_copy(own, gathered.at[core], store_sem.at[1])
    store_own.start()

    squares = jnp.where(diagonal_mask(), gram, 0.0)
    norm = jnp.sqrt(jnp.sum(jnp.sum(squares, axis=1, keepdims=True), axis=0, keepdims=True))
    scale = 1.0 / (norm + frob_eps)
    poly = newton_schulz(gram * scale * scale) * (scale * (0.2 * math.sqrt(D)))
    high, low = split(poly)
    poly_v[core, 0] = high
    poly_v[core, 1] = low
    norm_v[core] = jnp.broadcast_to(norm, (8, 128))
    polys = [
        remote(poly_v.at[core], poly_v.at[core], poly_send.at[0], poly_recv.at[0], sibling),
        remote(norm_v.at[core], norm_v.at[core], poly_send.at[1], poly_recv.at[1], sibling),
    ]
    for copy in polys:
        copy.start()

    theirs = 1 - core
    pltpu.make_async_copy(gathered.at[theirs], gathered.at[theirs], core_recv).wait()
    pltpu.make_async_copy(poly_v.at[theirs], poly_v.at[theirs], poly_recv.at[0]).wait()
    pltpu.make_async_copy(norm_v.at[theirs], norm_v.at[theirs], poly_recv.at[1]).wait()
    poly_out[...] = poly_v[...]
    norm_out[...] = norm_v[...]

    share_normed(lambda copy: copy.wait_send())

    def sent(m, _):
        share_grads(m, lambda copy: copy.wait_send())

        @pl.when(has_lower)
        def _():
            for j in range(len(PARTS)):
                chain_copy(2 * m, j).wait_send()
                chain_copy(2 * m + 1, j).wait_send()

        return 0

    lax.fori_loop(0, PAIRS, sent, 0)
    for copy in gives + ring_copies + core_copies + polys:
        copy.wait_send()
    store.wait()
    store_own.wait()


def backward(saved, top, w_down, w_up):
    hbm = pl.BlockSpec(memory_space=pl.ANY)
    vmem = pl.BlockSpec(memory_space=pltpu.VMEM)
    dma = pltpu.SemaphoreType.DMA
    return pl.pallas_call(
        backward_kernel,
        out_shape=(
            pltpu.VMEM((TOK, D), bf16),
            pltpu.VMEM((2, BLOCKS, LAT, BLOCK), bf16),
            pltpu.VMEM((2, 2, LAT, LAT), bf16),
            pltpu.VMEM((2, 8, 128), f32),
        ),
        in_specs=[hbm] * 4,
        out_specs=(hbm, hbm, vmem, vmem),
        scratch_shapes=[
            pltpu.VMEM((TOK, D), bf16),
            pltpu.VMEM((SMALLS, ROWS, PACK), bf16),
            pltpu.VMEM((LAT, D), bf16),
            pltpu.VMEM((LAT, D), bf16),
            pltpu.VMEM((PACK, 2 * LAT), bf16),
            pltpu.VMEM((TOK, D), bf16),
            pltpu.VMEM((TOK, D), bf16),
            pltpu.VMEM((SMALLS, ROWS, PACK), bf16),
            pltpu.VMEM((TOK, D), bf16),
            pltpu.VMEM((SMALLS, ROWS, PACK), bf16),
            pltpu.VMEM((TOK, 128), f32),
            pltpu.VMEM((TOK, LAT), f32),
            pltpu.VMEM((TOK, LAT), f32),
            pltpu.VMEM((TOK, LAT), bf16),
            pltpu.VMEM((TOK, LAT), bf16),
            pltpu.VMEM((PEERS, TOK, SPAN), bf16),
            pltpu.VMEM((PEERS, TOK, LAT), bf16),
            pltpu.VMEM((LAT, BLOCK), bf16),
            pltpu.VMEM((LAT, BLOCK), bf16),
            pltpu.VMEM((BLOCKS, LAT, BLOCK), bf16),
            pltpu.VMEM((2, 2, LAT, LAT), bf16),
            pltpu.VMEM((2, 8, 128), f32),
            dma((3,)),
            dma((BLOCKS,)),
            dma((SMALLS, len(PARTS))),
            dma((SMALLS, len(PARTS))),
            dma(()),
            dma((PEERS,)),
            dma(()),
            dma((PEERS,)),
            dma((2,)),
            dma((2,)),
            dma((2,)),
            dma((14,)),
            dma((BLOCKS, 2)),
            dma(()),
            dma(()),
            dma((2,)),
            dma((2,)),
        ],
        name="backward",
        compiler_params=pltpu.CompilerParams(
            collective_id=0, has_side_effects=True, vmem_limit_bytes=40 * 2**20
        ),
    )(saved, top, w_down, w_up)


def update_kernel(poly, block, norms, grads, out, norm_out, grads_out, stage, store_sem):
    stores = [pltpu.make_async_copy(grads, grads_out, store_sem.at[2 * BLOCKS])]
    stores[0].start()
    column = lax.broadcasted_iota(jnp.int32, (1, 2), 1)
    norm_out[...] = jnp.where(column == 0, norms[0, 0:1, 0:1], norms[1, 0:1, 0:1])
    for i in range(2):
        for j in range(BLOCKS):
            right = block[i, j]
            stage[i, j] = (dot(poly[i, 0], right) + dot(poly[i, 1], right)).astype(bf16)
            store = pltpu.make_async_copy(
                stage.at[i, j], out.at[0, i, :, pl.ds(j * BLOCK, BLOCK)], store_sem.at[i * BLOCKS + j]
            )
            store.start()
            stores.append(store)
    for store in stores:
        store.wait()


def update(poly, gathered, norms, grads):
    hbm = pl.BlockSpec(memory_space=pl.ANY)
    vmem = pl.BlockSpec(memory_space=pltpu.VMEM)
    return pl.pallas_call(
        update_kernel,
        out_shape=(
            jax.ShapeDtypeStruct((1, 2, LAT, D), bf16),
            jax.ShapeDtypeStruct((1, 2), f32),
            jax.ShapeDtypeStruct((TOK, D), bf16),
        ),
        in_specs=[vmem] * 4,
        out_specs=(hbm, vmem, hbm),
        scratch_shapes=[
            pltpu.VMEM((2, BLOCKS, LAT, BLOCK), bf16),
            pltpu.SemaphoreType.DMA((2 * BLOCKS + 1,)),
        ],
        name="update",
        compiler_params=pltpu.CompilerParams(vmem_limit_bytes=30 * 2**20),
    )(*[pltpu.with_memory_space_constraint(a, pltpu.VMEM) for a in (poly, gathered, norms, grads)])


def per_device(saved, top_grad, down_weight, up_weight):
    grads, gathered, poly, norms = backward(
        *[pltpu.with_memory_space_constraint(a, pltpu.HBM) for a in (saved[0], top_grad, down_weight[0], up_weight[0])]
    )
    updates, norm_values, grads = update(poly, gathered, norms, grads)
    return grads[None], updates, norm_values


def solution(mesh):
    return jax.shard_map(
        per_device,
        mesh=mesh,
        in_specs=(
            P("section", "dp", None),
            P("dp", None),
            P("section", None, None),
            P("section", None, None),
        ),
        out_specs=(P("section", "dp", None), P("section", None, None, None), P("section", None)),
        check_vma=False,
    )
```

profile of v0, /device:TPU:1, one launch (start us, length us, event | category | flops | bytes accessed | tf_op | source)
XLA Modules:
  0.0 147.3 jit_solution(15953138147906122548)
XLA Ops:
  0.6 140.5 %backward.1 = (bf16[128,7168]{1,0:T(8,128)(2,1)S(1)}, bf16[2,8,256,896]{3,2,1,0:T(8,128)(2,1)S(1)}, bf16[2,2,256,256]{3,2,1,0:T(8,128)(2,1)S(1)}, f32[2,8,128]{2,1,0:T(8,128)S(1)}) custom-call(bf16[128,7168]{1,0:T(8,128)(2,1)} %bitcast.6, bf16[128,7168]{1,0:T(8,128)(2,1)} %top.1, bf16[256,7168]{1,0:T(8,128)(2,1)} %bitcast.4, bf16[256,7168]{1,0:T(8,128)(2,1)} %bitcast.5), custom_call_target="tpu_custom_call" | custom-call | tf_op jit(solution)/shard_map/backward/pallas_call | solution.py:487
  141.1 6.0 %update.1 = (bf16[1,2,256,7168]{3,2,1,0:T(8,128)(2,1)}, f32[1,2]{1,0:T(1,128)}, bf16[128,7168]{1,0:T(8,128)(2,1)}) custom-call(bf16[2,2,256,256]{3,2,1,0:T(8,128)(2,1)S(1)} %get-tuple-element.10.poly, bf16[2,8,256,896]{3,2,1,0:T(8,128)(2,1)S(1)} %get-tuple-element.11.block, f32[2,8,128]{2,1,0:T(8,128)S(1)} %get-tuple-element.12.norms, ...), custom_call_target="tpu_custom_call" | custom-call | tf_op jit(solution)/shard_map/update/pallas_call | solution.py:566
where the time goes:
time: 147 us
  Pallas kernels  146 us (99%)
    pallas_call x1, Pallas kernels, backward(): pl.pallas_call(backward_kernel, out_shape=(pltpu.VMEM((TOK, D), bf16), pl...  140 us
    pallas_call x1, Pallas kernels, update(): pl.pallas_call(update_kernel, out_shape=(jax.ShapeDtypeStruct((1, 2, LAT,...  5.97 us

commit v1 on v0

v1 whole, which is shorter than its diff:
```python
import math

import jax
import jax.numpy as jnp
from jax import lax
from jax.experimental import pallas as pl
from jax.experimental.pallas import tpu as pltpu
from jax.sharding import PartitionSpec as P

D = 7168
LAT = 256
ITERS = 5
TOK = 128
ROWS = 16
PAIRS = TOK // ROWS
CHUNKS = 4
WIDE = D // CHUNKS
SMALL = 8
SMALLS = TOK // SMALL
PACK = D // 2
PARTS = ((0, 1024), (1024, 1024), (2048, 1024), (3072, 512))
QUARTERS = 4
READY = 3
QUARTER = LAT // QUARTERS
BLOCKS = 8
BLOCK = D // BLOCKS
PLACES = 8
PEERS = 16
Z = 4
SECTIONS = 8

norm_eps = 1e-06
frob_eps = 1e-07
coef_a = 3.4445
coef_b = -4.775
coef_c = 2.0315

MESH = pl.DeviceIdType.MESH
f32 = jnp.float32
bf16 = jnp.bfloat16
HIGHEST = lax.Precision.HIGHEST


def remote(src, dst, send, recv, device):
    return pltpu.make_async_remote_copy(
        src_ref=src, dst_ref=dst, send_sem=send, recv_sem=recv, device_id=device, device_id_type=MESH
    )


def nt_dot(a, b, precision=None):
    return lax.dot_general(
        a, b, (((1,), (1,)), ((), ())), preferred_element_type=f32, precision=precision
    )


def tn_dot(a, b):
    return lax.dot_general(a, b, (((0,), (0,)), ((), ())), preferred_element_type=f32)


def split(a):
    high = a.astype(bf16)
    return high, (a - high.astype(f32)).astype(bf16)


def dot(a, b):
    return jnp.dot(a, b, preferred_element_type=f32)


def exact_dot(a, b):
    return jnp.dot(a, b, precision=HIGHEST, preferred_element_type=f32)


def three_dot(a, b):
    (a_high, a_low), (b_high, b_low) = split(a), split(b)
    return dot(a_high, b_high) + (dot(a_high, b_low) + dot(a_low, b_high))


def newton_schulz(gram):
    total = None
    eye = diagonal_mask().astype(f32)
    for step in range(ITERS):
        mul = exact_dot if step < 1 else three_dot
        poly = coef_a * eye + coef_b * gram + coef_c * mul(gram, gram)
        if step < ITERS - 1:
            gram = mul(mul(poly, gram), poly)
        total = poly if total is None else three_dot(poly, total)
    return total


def diagonal_mask():
    return lax.broadcasted_iota(jnp.int32, (LAT, LAT), 0) == lax.broadcasted_iota(
        jnp.int32, (LAT, LAT), 1
    )


def backward_kernel(
    saved, top, w_down, w_up, grads_out, blocks, poly_out, norm_out,
    x_v, x_p, wd_v, wu_v, wut_v, normed_v, og_v, og_p, ig_v, ig_p, inv_v, latent_v, slope_v, act_v, lat_v,
    big_all, small_all, give_v, take_v,
    load_sem, wd_sem, chain_send, chain_recv, big_send, big_recv, small_send, small_recv, store_sem,
    give_send, give_recv, ring_send, ring_recv, core_send, core_recv, poly_send, poly_recv,
):
    s = lax.axis_index("section")
    d = lax.axis_index("dp")
    core = lax.rem(d, 2)
    q = lax.div(d, 2)
    x = lax.rem(q, 2)
    z = lax.div(q, 2)
    up = lax.rem(z + 1, Z)
    down = lax.rem(z + 3, Z)
    far = lax.rem(z + 2, Z)
    is_top = s == SECTIONS - 1
    has_lower = s > 0

    def device(z_at, x_at, core_at):
        return (s, z_at * 4 + x_at * 2 + core_at)

    across = device(z, 1 - x, core)
    above = device(up, x, core)
    below = device(down, x, core)
    sibling = device(z, x, 1 - core)

    loads = [
        pltpu.make_async_copy(saved, x_v, load_sem.at[0]),
        pltpu.make_async_copy(w_up, wu_v, load_sem.at[1]),
    ]
    for k in range(BLOCKS):
        part = pl.ds((k % 2) * PACK + (k // 2) * BLOCK, BLOCK)
        loads.append(
            pltpu.make_async_copy(w_down.at[:, pl.ds(k * BLOCK, BLOCK)], wd_v.at[:, part], wd_sem.at[k])
        )
    for load in loads:
        load.start()
    top_load = pltpu.make_async_copy(top, og_v, load_sem.at[2])

    @pl.when(is_top)
    def _():
        top_load.start()

    barrier = pltpu.get_barrier_semaphore()
    for k in range(1, PEERS):
        pl.semaphore_signal(
            barrier, inc=1, device_id=(s, lax.rem(d + k, PEERS)), device_id_type=MESH
        )

    @pl.when(jnp.logical_not(is_top))
    def _():
        pl.semaphore_signal(barrier, inc=1, device_id=(s + 1, d), device_id_type=MESH)

    def pack(flat, packed, i):
        rows = pl.ds(pl.multiple_of(i * ROWS, ROWS), ROWS)
        for k in range(Z):
            even = flat[rows, 2 * k * BLOCK:(2 * k + 1) * BLOCK].astype(f32)
            odd = flat[rows, (2 * k + 1) * BLOCK:(2 * k + 2) * BLOCK].astype(f32)
            cols = slice(k * BLOCK, (k + 1) * BLOCK)
            packed[2 * i, :, cols] = jnp.concatenate([even[:SMALL], odd[:SMALL]], axis=0).astype(bf16)
            packed[2 * i + 1, :, cols] = jnp.concatenate([even[SMALL:], odd[SMALL:]], axis=0).astype(bf16)

    def unpack(packed, flat, i):
        rows = pl.ds(pl.multiple_of(i * ROWS, ROWS), ROWS)
        for k in range(Z):
            cols = slice(k * BLOCK, (k + 1) * BLOCK)
            first = packed[2 * i, :, cols].astype(f32)
            second = packed[2 * i + 1, :, cols].astype(f32)
            even = jnp.concatenate([first[:SMALL], second[:SMALL]], axis=0)
            odd = jnp.concatenate([first[SMALL:], second[SMALL:]], axis=0)
            flat[rows, 2 * k * BLOCK:(2 * k + 1) * BLOCK] = even.astype(bf16)
            flat[rows, (2 * k + 1) * BLOCK:(2 * k + 2) * BLOCK] = odd.astype(bf16)

    loads[0].wait()

    def norm_rows(m, _):
        rows = pl.ds(pl.multiple_of(m * ROWS, ROWS), ROWS)
        total = jnp.zeros((ROWS, 1), f32)
        for j in range(CHUNKS):
            part = x_v[rows, j * WIDE:(j + 1) * WIDE].astype(f32)
            total += jnp.sum(part * part, axis=1, keepdims=True)
        inv = 1.0 / jnp.sqrt(total * (1.0 / D) + norm_eps)
        inv_v[rows, :] = jnp.broadcast_to(inv, (ROWS, 128))
        for j in range(CHUNKS):
            part = x_v[rows, j * WIDE:(j + 1) * WIDE].astype(f32)
            normed_v[rows, j * WIDE:(j + 1) * WIDE] = (part * inv).astype(bf16)
        return 0

    lax.fori_loop(0, PAIRS, norm_rows, 0)
    loads[1].wait()

    def turn(k, _):
        for odd in range(2):
            cols = pl.ds(pl.multiple_of((2 * k + odd) * BLOCK, BLOCK), BLOCK)
            rows = pl.ds(pl.multiple_of(k * BLOCK, BLOCK), BLOCK)
            wut_v[rows, odd * LAT:(odd + 1) * LAT] = wu_v[:, cols].T
        return 0

    lax.fori_loop(0, Z, turn, 0)
    for load in loads[2:]:
        load.wait()

    def latent_part(k, acc):
        for odd in range(2):
            cols = pl.ds(pl.multiple_of((2 * k + odd) * BLOCK, BLOCK), BLOCK)
            part = pl.ds(pl.multiple_of(odd * PACK + k * BLOCK, BLOCK), BLOCK)
            acc = acc + nt_dot(normed_v[:, cols], wd_v[:, part])
        return acc

    latent = lax.fori_loop(0, Z, latent_part, jnp.zeros((TOK, LAT), f32))
    sigmoid = 1.0 / (1.0 + jnp.exp(-latent))
    latent_v[...] = latent
    act_v[...] = (latent * sigmoid).astype(bf16)
    slope_v[...] = sigmoid * (1.0 + latent * (1.0 - sigmoid))

    @pl.when(has_lower)
    def _():
        pl.semaphore_wait(barrier, PEERS)

    @pl.when(jnp.logical_not(has_lower))
    def _():
        pl.semaphore_wait(barrier, PEERS - 1)

    place = z * 2 + core
    direct = s == 0

    def share_block(src_of, rows, target_core, act, act_own):
        for k in range(Z):
            z_at = lax.rem(z + k, Z)
            for e in range(2):
                half = lax.rem(x + e, 2)
                to_x = jnp.where(direct, half, x)
                slot = jnp.where(direct, x, half)
                src = src_of(pl.ds(pl.multiple_of((z_at * 2 + half) * BLOCK, BLOCK), BLOCK))
                dst = big_all.at[place, slot, rows]
                recv = big_recv.at[place, slot]
                copy = remote(src, dst, big_send, recv, device(z_at, to_x, target_core))
                if k:
                    act(copy)
                else:
                    away = core != target_core
                    if e:
                        away = jnp.logical_or(away, direct)

                    @pl.when(away)
                    def _():
                        act(copy)

                    if act_own is not None:

                        @pl.when(jnp.logical_not(away))
                        def _():
                            act_own(pltpu.make_async_copy(src, dst, recv))

    def share_small(src, rows, target_core, act, act_own):
        slot = jnp.where(direct, x, 0)
        dst = small_all.at[place, slot, rows]
        recv = small_recv.at[place, slot]
        for k in range(Z):
            z_at = lax.rem(z + k, Z)
            copy = remote(src, dst, small_send, recv, device(z_at, x, target_core))
            if k:
                act(copy)
            else:

                @pl.when(core != target_core)
                def _():
                    act(copy)

                if act_own is not None:

                    @pl.when(core == target_core)
                    def _():
                        act_own(pltpu.make_async_copy(src, dst, recv))

        @pl.when(direct)
        def _():
            for k in range(Z):
                z_at = lax.rem(z + k, Z)
                act(remote(src, dst, small_send, recv, device(z_at, 1 - x, target_core)))

    def begin(copy):
        copy.start()

    def left(copy):
        copy.wait_send()

    every = pl.ds(0, TOK)

    def share_normed(act, act_own):
        share_block(lambda cols: normed_v.at[:, cols], every, 0, act, act_own)
        share_small(act_v, every, 1, act, act_own)

    def share_grads(i, act, act_own):
        rows = pl.ds(pl.multiple_of(i * ROWS, ROWS), ROWS)
        share_block(lambda cols: og_v.at[rows, cols], rows, 1, act, act_own)
        share_small(lat_v.at[rows], rows, 0, act, act_own)

    @pl.when(jnp.logical_not(is_top))
    def _():
        share_normed(begin, begin)

    @pl.when(is_top)
    def _():
        top_load.wait()

    def chain_copy(m, j):
        cols = pl.ds(*PARTS[j])
        return remote(
            ig_p.at[m, :, cols], og_p.at[m, :, cols], chain_send.at[m, j], chain_recv.at[m, j],
            (jnp.maximum(s - 1, 0), d),
        )

    def receive(m):
        rows = pl.ds(pl.multiple_of(m * SMALL, SMALL), SMALL)
        acc = jnp.zeros((ROWS, 2 * LAT), f32)
        for j, (at, width) in enumerate(PARTS):

            @pl.when(jnp.logical_not(is_top))
            def _():
                chain_copy(m, j).wait_recv()

            acc += dot(og_p[m, :, at:at + width], wut_v[at:at + width, :])
        act_grad = acc[:SMALL, :LAT] + acc[SMALL:, LAT:]
        lat = (act_grad * slope_v[rows, :]).astype(bf16).astype(f32)
        inv = inv_v[rows, 0:1]
        mean = jnp.sum(lat * latent_v[rows, :], axis=1, keepdims=True) * (1.0 / D)
        pull = inv * inv * mean
        return lat, inv, pull

    def answer(m, lat, inv, pull):
        lat_twice = jnp.concatenate([lat, lat], axis=0).astype(bf16)
        inv_twice = jnp.concatenate([inv, inv], axis=0)
        pull_twice = jnp.concatenate([pull, pull], axis=0)
        for j, (at, width) in enumerate(PARTS):
            cols = slice(at, at + width)
            even = dot(lat_twice, wd_v[:, at:at + width])
            odd = dot(lat_twice, wd_v[:, PACK + at:PACK + at + width])
            ng = jnp.concatenate([even[:SMALL], odd[SMALL:]], axis=0)
            out = og_p[m, :, cols].astype(f32) + inv_twice * ng - pull_twice * x_p[m, :, cols].astype(f32)
            ig_p[m, :, cols] = out.astype(bf16)

            @pl.when(has_lower)
            def _():
                chain_copy(m, j).start()

    def micro(i, _):
        rows = pl.ds(pl.multiple_of(i * ROWS, ROWS), ROWS)
        pack(x_v, x_p, i)

        @pl.when(is_top)
        def _():
            pack(og_v, og_p, i)

        first = receive(2 * i)
        answer(2 * i, *first)
        second = receive(2 * i + 1)

        def share_pair():
            lat_v[rows, :] = jnp.concatenate([first[0], second[0]], axis=0).astype(bf16)

            @pl.when(jnp.logical_not(is_top))
            def _():
                unpack(og_p, og_v, i)

            share_grads(i, begin, begin)

        @pl.when(direct)
        def _():
            share_pair()

        answer(2 * i + 1, *second)

        @pl.when(jnp.logical_not(direct))
        def _():
            share_pair()

        unpack(ig_p, ig_v, i)
        return 0

    lax.fori_loop(0, PAIRS, micro, 0)

    @pl.when(is_top)
    def _():
        share_normed(begin, begin)

    store = pltpu.make_async_copy(ig_v, grads_out, store_sem)
    store.start()

    def arrived(p, _):
        for slot in range(2):
            part = big_all.at[p, slot]
            pltpu.make_async_copy(part, part, big_recv.at[p, slot]).wait()
        part = small_all.at[p, 0]
        pltpu.make_async_copy(part, part, small_recv.at[p, 0]).wait()
        return 0

    lax.fori_loop(0, PLACES, arrived, 0)

    @pl.when(direct)
    def _():
        def more(p, _):
            part = small_all.at[p, 1]
            pltpu.make_async_copy(part, part, small_recv.at[p, 1]).wait()
            return 0

        lax.fori_loop(0, PLACES, more, 0)

    ring_copies = []
    core_copies = []

    def quarter_rows(n):
        return pl.ds(n * QUARTER, QUARTER)

    def at(z_at, x_at, n):
        return blocks.at[core, z_at * 2 + x_at, quarter_rows(n)]

    def ring_copy(z_at, x_at, n, to, sem):
        return remote(
            at(z_at, x_at, n), at(z_at, x_at, n), ring_send.at[sem], ring_recv.at[z_at * 2 + x_at, n], to
        )

    def forward(z_at, x_at, n, to):
        copy = ring_copy(z_at, x_at, n, to, 3 * QUARTERS + len(ring_copies))
        copy.start()
        ring_copies.append(copy)

    def core_copy(z_at, x_at, n):
        return remote(
            at(z_at, x_at, n), at(z_at, x_at, n), core_send, core_recv, sibling
        )

    def to_sibling(z_at, x_at, n):
        copy = core_copy(z_at, x_at, n)
        copy.start()
        core_copies.append(copy)

    def wait(z_at, x_at, n):
        part = at(z_at, x_at, n)
        pltpu.make_async_copy(part, part, ring_recv.at[z_at * 2 + x_at, n]).wait()

    def used(z_at, x_at):
        part = blocks[core, z_at * 2 + x_at]
        return nt_dot(part, part)

    def own_copies(n):
        return [ring_copy(z, x, n, to, 3 * n + k) for k, to in enumerate((above, below, across))] + [
            core_copy(z, x, n)
        ]

    def send_own(n):
        for copy in own_copies(n):
            copy.start()

    @pl.when(direct)
    def _():
        turned = small_all[...].reshape(2 * PLACES * TOK, LAT).T
        right = big_all[...].reshape(2 * PLACES * TOK, BLOCK)
        for n in range(QUARTERS):
            blocks[core, q, quarter_rows(n)] = dot(turned[n * QUARTER:(n + 1) * QUARTER], right).astype(bf16)
            send_own(n)

    def give_copy(n):
        return remote(
            give_v.at[quarter_rows(n)], take_v.at[quarter_rows(n)], give_send.at[n], give_recv.at[n], across
        )

    @pl.when(jnp.logical_not(direct))
    def _():
        turned = small_all[:, 0].reshape(PLACES * TOK, LAT).T
        right = big_all[:, 1 - x].reshape(PLACES * TOK, BLOCK)
        for n in range(QUARTERS):
            give_v[quarter_rows(n)] = dot(turned[n * QUARTER:(n + 1) * QUARTER], right).astype(bf16)
            give_copy(n).start()
        mine = dot(turned, big_all[:, x].reshape(PLACES * TOK, BLOCK))
        for n in range(QUARTERS):
            give_copy(n).wait_recv()
            total = mine[n * QUARTER:(n + 1) * QUARTER] + take_v[quarter_rows(n)].astype(f32)
            blocks[core, q, quarter_rows(n)] = total.astype(bf16)
            send_own(n)
        for n in range(QUARTERS):
            give_copy(n).wait_send()

    gram = used(z, x)
    for n in range(QUARTERS):
        wait(down, x, n)
        if n < QUARTERS // 2:
            forward(down, x, n, above)
        to_sibling(down, x, n)
        wait(up, x, n)
        if n >= QUARTERS // 2:
            forward(up, x, n, below)
        to_sibling(up, x, n)
        wait(z, 1 - x, n)
        forward(z, 1 - x, n, above)
        forward(z, 1 - x, n, below)
        to_sibling(z, 1 - x, n)
    gram += used(down, x)
    gram += used(up, x)
    gram += used(z, 1 - x)
    for n in (0, 2, 1, 3):
        wait(far, x, n)
        forward(far, x, n, across)
        to_sibling(far, x, n)
    gram += used(far, x)
    for n in range(QUARTERS):
        for z_at in (up, down):
            wait(z_at, 1 - x, n)
            to_sibling(z_at, 1 - x, n)
    gram += used(up, 1 - x)
    gram += used(down, 1 - x)
    for n in (0, 2, 1, 3):
        wait(far, 1 - x, n)
        to_sibling(far, 1 - x, n)
    gram += used(far, 1 - x)

    squares = jnp.where(diagonal_mask(), gram, 0.0)
    norm = jnp.sqrt(jnp.sum(jnp.sum(squares, axis=1, keepdims=True), axis=0, keepdims=True))
    scale = 1.0 / (norm + frob_eps)
    poly = newton_schulz(gram * scale * scale) * (scale * (0.2 * math.sqrt(D)))
    high, low = split(poly)
    poly_out[core, 0] = high
    poly_out[core, 1] = low
    norm_out[core] = jnp.broadcast_to(norm, (8, 128))
    polys = [
        remote(poly_out.at[core], poly_out.at[core], poly_send.at[0], poly_recv.at[0], sibling),
        remote(norm_out.at[core], norm_out.at[core], poly_send.at[1], poly_recv.at[1], sibling),
    ]
    for copy in polys:
        copy.start()

    for n in range(QUARTERS):
        for copy in own_copies(n):
            copy.wait_send()
    for copy in ring_copies + core_copies:
        copy.wait_send()

    def finish(j, _):
        right = blocks[core, j]
        blocks[core, j] = (dot(high, right) + dot(low, right)).astype(bf16)
        return 0

    lax.fori_loop(0, READY, finish, 0)
    theirs = 1 - core
    pltpu.make_async_copy(blocks.at[theirs], blocks.at[theirs], core_recv).wait()
    pltpu.make_async_copy(poly_out.at[theirs], poly_out.at[theirs], poly_recv.at[0]).wait()
    pltpu.make_async_copy(norm_out.at[theirs], norm_out.at[theirs], poly_recv.at[1]).wait()

    share_normed(left, None)

    def sent(m, _):
        share_grads(m, left, None)

        @pl.when(has_lower)
        def _():
            for j in range(len(PARTS)):
                chain_copy(2 * m, j).wait_send()
                chain_copy(2 * m + 1, j).wait_send()

        return 0

    lax.fori_loop(0, PAIRS, sent, 0)
    for copy in polys:
        copy.wait_send()
    store.wait()


def backward(saved, top, w_down, w_up):
    hbm = pl.BlockSpec(memory_space=pl.ANY)
    vmem = pl.BlockSpec(memory_space=pltpu.VMEM)
    dma = pltpu.SemaphoreType.DMA
    return pl.pallas_call(
        backward_kernel,
        out_shape=(
            pltpu.VMEM((TOK, D), bf16),
            pltpu.VMEM((2, BLOCKS, LAT, BLOCK), bf16),
            pltpu.VMEM((2, 2, LAT, LAT), bf16),
            pltpu.VMEM((2, 8, 128), f32),
        ),
        in_specs=[hbm] * 4,
        out_specs=(hbm, vmem, vmem, vmem),
        scratch_shapes=[
            pltpu.VMEM((TOK, D), bf16),
            pltpu.VMEM((SMALLS, ROWS, PACK), bf16),
            pltpu.VMEM((LAT, D), bf16),
            pltpu.VMEM((LAT, D), bf16),
            pltpu.VMEM((PACK, 2 * LAT), bf16),
            pltpu.VMEM((TOK, D), bf16),
            pltpu.VMEM((TOK, D), bf16),
            pltpu.VMEM((SMALLS, ROWS, PACK), bf16),
            pltpu.VMEM((TOK, D), bf16),
            pltpu.VMEM((SMALLS, ROWS, PACK), bf16),
            pltpu.VMEM((TOK, 128), f32),
            pltpu.VMEM((TOK, LAT), f32),
            pltpu.VMEM((TOK, LAT), f32),
            pltpu.VMEM((TOK, LAT), bf16),
            pltpu.VMEM((TOK, LAT), bf16),
            pltpu.VMEM((PLACES, 2, TOK, BLOCK), bf16),
            pltpu.VMEM((PLACES, 2, TOK, LAT), bf16),
            pltpu.VMEM((LAT, BLOCK), bf16),
            pltpu.VMEM((LAT, BLOCK), bf16),
            dma((3,)),
            dma((BLOCKS,)),
            dma((SMALLS, len(PARTS))),
            dma((SMALLS, len(PARTS))),
            dma(()),
            dma((PLACES, 2)),
            dma(()),
            dma((PLACES, 2)),
            dma(()),
            dma((QUARTERS,)),
            dma((QUARTERS,)),
            dma((7 * QUARTERS,)),
            dma((BLOCKS, QUARTERS)),
            dma(()),
            dma(()),
            dma((2,)),
            dma((2,)),
        ],
        name="backward",
        compiler_params=pltpu.CompilerParams(
            collective_id=0, has_side_effects=True, vmem_limit_bytes=40 * 2**20
        ),
    )(saved, top, w_down, w_up)


def update_kernel(poly, blocks, norms, grads, out, norm_out, grads_out, stage, store_sem):
    mine = lax.rem(lax.axis_index("dp"), 2)
    theirs = 1 - mine
    stores = []

    def store(src, dst):
        copy = pltpu.make_async_copy(src, dst, store_sem.at[len(stores)])
        copy.start()
        stores.append(copy)

    for j in range(READY):
        store(blocks.at[mine, j], out.at[0, mine, :, pl.ds(j * BLOCK, BLOCK)])
    store(grads, grads_out)
    column = lax.broadcasted_iota(jnp.int32, (1, 2), 1)
    norm_out[...] = jnp.where(column == 0, norms[0, 0:1, 0:1], norms[1, 0:1, 0:1])
    todo = [(mine, j) for j in range(READY, BLOCKS)] + [(theirs, j) for j in range(BLOCKS)]
    for n, (i, j) in enumerate(todo):
        right = blocks[i, j]
        stage[n] = (dot(poly[i, 0], right) + dot(poly[i, 1], right)).astype(bf16)
        store(stage.at[n], out.at[0, i, :, pl.ds(j * BLOCK, BLOCK)])
    for copy in stores:
        copy.wait()


def update(poly, blocks, norms, grads):
    hbm = pl.BlockSpec(memory_space=pl.ANY)
    vmem = pl.BlockSpec(memory_space=pltpu.VMEM)
    return pl.pallas_call(
        update_kernel,
        out_shape=(
            jax.ShapeDtypeStruct((1, 2, LAT, D), bf16),
            jax.ShapeDtypeStruct((1, 2), f32),
            jax.ShapeDtypeStruct((TOK, D), bf16),
        ),
        in_specs=[vmem] * 4,
        out_specs=(hbm, vmem, hbm),
        scratch_shapes=[
            pltpu.VMEM((2 * BLOCKS - READY, LAT, BLOCK), bf16),
            pltpu.SemaphoreType.DMA((2 * BLOCKS + 1,)),
        ],
        name="update",
        compiler_params=pltpu.CompilerParams(vmem_limit_bytes=30 * 2**20),
    )(*[pltpu.with_memory_space_constraint(a, pltpu.VMEM) for a in (poly, blocks, norms, grads)])


def per_device(saved, top_grad, down_weight, up_weight):
    grads, blocks, poly, norms = backward(
        *[pltpu.with_memory_space_constraint(a, pltpu.HBM) for a in (saved[0], top_grad, down_weight[0], up_weight[0])]
    )
    updates, norm_values, grads = update(poly, blocks, norms, grads)
    return grads[None], updates, norm_values


def solution(mesh):
    return jax.shard_map(
        per_device,
        mesh=mesh,
        in_specs=(
            P("section", "dp", None),
            P("dp", None),
            P("section", None, None),
            P("section", None, None),
        ),
        out_specs=(P("section", "dp", None), P("section", None, None, None), P("section", None)),
        check_vma=False,
    )
```

time: 147 us -> 140 us (0.952)
  Pallas kernels: 146 us -> 139 us
    pallas_call x1, Pallas kernels: 140 us -> 134 us  [backward(): pl.pallas_call(backward_kernel, out_shape=(pltpu.VMEM((TOK, D), bf16), pl...]
where the time goes in v1:
time: 140 us
  Pallas kernels  139 us (99%)
    pallas_call x1, Pallas kernels, backward(): pl.pallas_call(backward_kernel, out_shape=(pltpu.VMEM((TOK, D), bf16), pl...  134 us
    pallas_call x1, Pallas kernels, update(): pl.pallas_call(update_kernel, out_shape=(jax.ShapeDtypeStruct((1, 2, LAT,...  5.16 us

profile of v1, /device:TPU:1, one launch (start us, length us, event | category | flops | bytes accessed | tf_op | source)
XLA Modules:
  0.0 140.2 jit_solution(17130854427929027727)
XLA Ops:
  0.6 134.2 %backward.1 = (bf16[128,7168]{1,0:T(8,128)(2,1)S(1)}, bf16[2,8,256,896]{3,2,1,0:T(8,128)(2,1)S(1)}, bf16[2,2,256,256]{3,2,1,0:T(8,128)(2,1)S(1)}, f32[2,8,128]{2,1,0:T(8,128)S(1)}) custom-call(bf16[128,7168]{1,0:T(8,128)(2,1)} %bitcast.6, bf16[128,7168]{1,0:T(8,128)(2,1)} %top.1, bf16[256,7168]{1,0:T(8,128)(2,1)} %bitcast.4, bf16[256,7168]{1,0:T(8,128)(2,1)} %bitcast.5), custom_call_target="tpu_custom_call" | custom-call | tf_op jit(solution)/shard_map/backward/pallas_call | solution.py:568
  134.9 5.2 %update.1 = (bf16[1,2,256,7168]{3,2,1,0:T(8,128)(2,1)}, f32[1,2]{1,0:T(1,128)}, bf16[128,7168]{1,0:T(8,128)(2,1)}) custom-call(bf16[2,2,256,256]{3,2,1,0:T(8,128)(2,1)S(1)} %get-tuple-element.10.poly, bf16[2,8,256,896]{3,2,1,0:T(8,128)(2,1)S(1)} %get-tuple-element.11.blocks, f32[2,8,128]{2,1,0:T(8,128)S(1)} %get-tuple-element.12.norms, ...), custom_call_target="tpu_custom_call" | custom-call | tf_op jit(solution)/shard_map/update/pallas_call | solution.py:650

commit v2 on v1

--- a/solution.py
+++ b/solution.py
@@ -9,6 +9,7 @@
 
 D = 7168
 LAT = 256
+SECTIONS = 8
 ITERS = 5
 TOK = 128
 ROWS = 16
@@ -19,15 +20,18 @@
 SMALLS = TOK // SMALL
 PACK = D // 2
 PARTS = ((0, 1024), (1024, 1024), (2048, 1024), (3072, 512))
-QUARTERS = 4
 READY = 3
-QUARTER = LAT // QUARTERS
+PIECES = ((0, 64), (64, 64), (128, 80), (208, 48))
+QUARTERS = len(PIECES)
+LAST = QUARTERS - 1
+ORDER = (LAST, 0, 1, 2)
+HELPED = 2
+APART = SECTIONS - HELPED
 BLOCKS = 8
 BLOCK = D // BLOCKS
 PLACES = 8
 PEERS = 16
 Z = 4
-SECTIONS = 8
 
 norm_eps = 1e-06
 frob_eps = 1e-07
@@ -38,7 +42,6 @@
 MESH = pl.DeviceIdType.MESH
 f32 = jnp.float32
 bf16 = jnp.bfloat16
-HIGHEST = lax.Precision.HIGHEST
 
 
 def remote(src, dst, send, recv, device):
@@ -47,9 +50,9 @@
     )
 
 
-def nt_dot(a, b, precision=None):
+def nt_dot(a, b):
     return lax.dot_general(
-        a, b, (((1,), (1,)), ((), ())), preferred_element_type=f32, precision=precision
+        a, b, (((1,), (1,)), ((), ())), preferred_element_type=f32
     )
 
 
@@ -64,10 +67,6 @@
 
 def dot(a, b):
     return jnp.dot(a, b, preferred_element_type=f32)
-
-
-def exact_dot(a, b):
-    return jnp.dot(a, b, precision=HIGHEST, preferred_element_type=f32)
 
 
 def three_dot(a, b):
@@ -79,10 +78,9 @@
     total = None
     eye = diagonal_mask().astype(f32)
     for step in range(ITERS):
-        mul = exact_dot if step < 1 else three_dot
-        poly = coef_a * eye + coef_b * gram + coef_c * mul(gram, gram)
+        poly = coef_a * eye + coef_b * gram + coef_c * three_dot(gram, gram)
         if step < ITERS - 1:
-            gram = mul(mul(poly, gram), poly)
+            gram = three_dot(three_dot(poly, gram), poly)
         total = poly if total is None else three_dot(poly, total)
     return total
 
@@ -96,9 +94,9 @@
 def backward_kernel(
     saved, top, w_down, w_up, grads_out, blocks, poly_out, norm_out,
     x_v, x_p, wd_v, wu_v, wut_v, normed_v, og_v, og_p, ig_v, ig_p, inv_v, latent_v, slope_v, act_v, lat_v,
-    big_all, small_all, give_v, take_v,
+    big_all, small_all, give_v, take_v, relay,
     load_sem, wd_sem, chain_send, chain_recv, big_send, big_recv, small_send, small_recv, store_sem,
-    give_send, give_recv, ring_send, ring_recv, core_send, core_recv, poly_send, poly_recv,
+    give_send, give_recv, ring_send, ring_recv, core_send, core_recv, poly_send, poly_recv, relay_send, relay_recv,
 ):
     s = lax.axis_index("section")
     d = lax.axis_index("dp")
@@ -167,6 +165,14 @@
             flat[rows, 2 * k * BLOCK:(2 * k + 1) * BLOCK] = even.astype(bf16)
             flat[rows, (2 * k + 1) * BLOCK:(2 * k + 2) * BLOCK] = odd.astype(bf16)
 
+    helped = s < HELPED
+    helper = s >= APART
+    partner = (jnp.where(helped, s + APART, jnp.where(helper, s - APART, s)), d)
+
+    @pl.when(jnp.logical_or(helped, helper))
+    def _():
+        pl.semaphore_signal(barrier, inc=1, device_id=partner, device_id_type=MESH)
+
     loads[0].wait()
 
     def norm_rows(m, _):
@@ -209,13 +215,15 @@
     act_v[...] = (latent * sigmoid).astype(bf16)
     slope_v[...] = sigmoid * (1.0 + latent * (1.0 - sigmoid))
 
-    @pl.when(has_lower)
+    both = jnp.logical_and(has_lower, jnp.logical_or(helped, helper))
+
+    @pl.when(both)
+    def _():
+        pl.semaphore_wait(barrier, PEERS + 1)
+
+    @pl.when(jnp.logical_not(both))
     def _():
         pl.semaphore_wait(barrier, PEERS)
-
-    @pl.when(jnp.logical_not(has_lower))
-    def _():
-        pl.semaphore_wait(barrier, PEERS - 1)
 
     place = z * 2 + core
     direct = s == 0
@@ -348,6 +356,10 @@
         def _():
             pack(og_v, og_p, i)
 
+        @pl.when(jnp.logical_and(is_top, i == 1))
+        def _():
+            share_normed(begin, begin)
+
         first = receive(2 * i)
         answer(2 * i, *first)
         second = receive(2 * i + 1)
@@ -375,10 +387,6 @@
         return 0
 
     lax.fori_loop(0, PAIRS, micro, 0)
-
-    @pl.when(is_top)
-    def _():
-        share_normed(begin, begin)
 
     store = pltpu.make_async_copy(ig_v, grads_out, store_sem)
     store.start()
@@ -403,10 +411,14 @@
         lax.fori_loop(0, PLACES, more, 0)
 
     ring_copies = []
+    alone_copies = []
     core_copies = []
 
     def quarter_rows(n):
-        return pl.ds(n * QUARTER, QUARTER)
+        return pl.ds(*PIECES[n])
+
+    def piece(n):
+        return slice(PIECES[n][0], PIECES[n][0] + PIECES[n][1])
 
     def at(z_at, x_at, n):
         return blocks.at[core, z_at * 2 + x_at, quarter_rows(n)]
@@ -417,9 +429,16 @@
         )
 
     def forward(z_at, x_at, n, to):
-        copy = ring_copy(z_at, x_at, n, to, 3 * QUARTERS + len(ring_copies))
-        copy.start()
-        ring_copies.append(copy)
+        copy = ring_copy(z_at, x_at, n, to, 3 * QUARTERS + len(ring_copies) + len(alone_copies))
+        if n == LAST:
+            alone_copies.append(copy)
+
+            @pl.when(jnp.logical_not(helped))
+            def _():
+                copy.start()
+        else:
+            copy.start()
+            ring_copies.append(copy)
 
     def core_copy(z_at, x_at, n):
         return remote(
@@ -439,22 +458,30 @@
         part = blocks[core, z_at * 2 + x_at]
         return nt_dot(part, part)
 
-    def own_copies(n):
-        return [ring_copy(z, x, n, to, 3 * n + k) for k, to in enumerate((above, below, across))] + [
-            core_copy(z, x, n)
-        ]
-
-    def send_own(n):
-        for copy in own_copies(n):
-            copy.start()
+    def own_copies(n, act):
+        copies = [ring_copy(z, x, n, to, 3 * n + k) for k, to in enumerate((above, below, across))]
+        act(core_copy(z, x, n))
+        if n != LAST:
+            for copy in copies:
+                act(copy)
+        else:
+
+            @pl.when(jnp.logical_not(helped))
+            def _():
+                for copy in copies:
+                    act(copy)
+
+            @pl.when(helped)
+            def _():
+                act(remote(at(z, x, n), relay.at[q], relay_send.at[0], relay_recv.at[q], partner))
 
     @pl.when(direct)
     def _():
         turned = small_all[...].reshape(2 * PLACES * TOK, LAT).T
         right = big_all[...].reshape(2 * PLACES * TOK, BLOCK)
-        for n in range(QUARTERS):
-            blocks[core, q, quarter_rows(n)] = dot(turned[n * QUARTER:(n + 1) * QUARTER], right).astype(bf16)
-            send_own(n)
+        for n in ORDER:
+            blocks[core, q, quarter_rows(n)] = dot(turned[piece(n)], right).astype(bf16)
+            own_copies(n, begin)
 
     def give_copy(n):
         return remote(
@@ -465,20 +492,19 @@
     def _():
         turned = small_all[:, 0].reshape(PLACES * TOK, LAT).T
         right = big_all[:, 1 - x].reshape(PLACES * TOK, BLOCK)
-        for n in range(QUARTERS):
-            give_v[quarter_rows(n)] = dot(turned[n * QUARTER:(n + 1) * QUARTER], right).astype(bf16)
+        for n in ORDER:
+            give_v[quarter_rows(n)] = dot(turned[piece(n)], right).astype(bf16)
             give_copy(n).start()
         mine = dot(turned, big_all[:, x].reshape(PLACES * TOK, BLOCK))
-        for n in range(QUARTERS):
+        for n in ORDER:
             give_copy(n).wait_recv()
-            total = mine[n * QUARTER:(n + 1) * QUARTER] + take_v[quarter_rows(n)].astype(f32)
+            total = mine[piece(n)] + take_v[quarter_rows(n)].astype(f32)
             blocks[core, q, quarter_rows(n)] = total.astype(bf16)
-            send_own(n)
+            own_copies(n, begin)
         for n in range(QUARTERS):
             give_copy(n).wait_send()
 
-    gram = used(z, x)
-    for n in range(QUARTERS):
+    def near(n):
         wait(down, x, n)
         if n < QUARTERS // 2:
             forward(down, x, n, above)
@@ -491,13 +517,22 @@
         forward(z, 1 - x, n, above)
         forward(z, 1 - x, n, below)
         to_sibling(z, 1 - x, n)
+
+    def opposite(n):
+        wait(far, x, n)
+        forward(far, x, n, across)
+        to_sibling(far, x, n)
+
+    gram = used(z, x)
+    for n in range(LAST):
+        near(n)
+    for n in (0, 2, 1):
+        opposite(n)
+    near(LAST)
+    opposite(LAST)
     gram += used(down, x)
     gram += used(up, x)
     gram += used(z, 1 - x)
-    for n in (0, 2, 1, 3):
-        wait(far, x, n)
-        forward(far, x, n, across)
-        to_sibling(far, x, n)
     gram += used(far, x)
     for n in range(QUARTERS):
         for z_at in (up, down):
@@ -526,10 +561,14 @@
         copy.start()
 
     for n in range(QUARTERS):
-        for copy in own_copies(n):
-            copy.wait_send()
+        own_copies(n, left)
     for copy in ring_copies + core_copies:
         copy.wait_send()
+
+    @pl.when(jnp.logical_not(helped))
+    def _():
+        for copy in alone_copies:
+            copy.wait_send()
 
     def finish(j, _):
         right = blocks[core, j]
@@ -541,6 +580,51 @@
     pltpu.make_async_copy(blocks.at[theirs], blocks.at[theirs], core_recv).wait()
     pltpu.make_async_copy(poly_out.at[theirs], poly_out.at[theirs], poly_recv.at[0]).wait()
     pltpu.make_async_copy(norm_out.at[theirs], norm_out.at[theirs], poly_recv.at[1]).wait()
+
+    @pl.when(helper)
+    def _():
+        relays = []
+
+        def pass_to(z_at, x_at, to):
+            n = z_at * 2 + x_at
+            copy = remote(relay.at[n], relay.at[n], relay_send.at[len(relays)], relay_recv.at[n], to)
+            copy.start()
+            relays.append(copy)
+
+        def arrive(z_at, x_at):
+            n = z_at * 2 + x_at
+            pltpu.make_async_copy(relay.at[n], relay.at[n], relay_recv.at[n]).wait()
+
+        def deliver(z_at, x_at):
+            n = z_at * 2 + x_at
+            copy = remote(
+                relay.at[n], blocks.at[core, n, quarter_rows(LAST)],
+                relay_send.at[len(relays)], ring_recv.at[n, LAST], partner,
+            )
+            copy.start()
+            relays.append(copy)
+
+        arrive(z, x)
+        pass_to(z, x, above)
+        pass_to(z, x, below)
+        pass_to(z, x, across)
+        arrive(down, x)
+        pass_to(down, x, above)
+        deliver(down, x)
+        arrive(up, x)
+        deliver(up, x)
+        arrive(z, 1 - x)
+        pass_to(z, 1 - x, above)
+        pass_to(z, 1 - x, below)
+        deliver(z, 1 - x)
+        arrive(far, x)
+        pass_to(far, x, across)
+        deliver(far, x)
+        for z_at in (up, down, far):
+            arrive(z_at, 1 - x)
+            deliver(z_at, 1 - x)
+        for copy in relays:
+            copy.wait_send()
 
     share_normed(left, None)
 
@@ -595,6 +679,7 @@
             pltpu.VMEM((PLACES, 2, TOK, LAT), bf16),
             pltpu.VMEM((LAT, BLOCK), bf16),
             pltpu.VMEM((LAT, BLOCK), bf16),
+            pltpu.VMEM((BLOCKS, PIECES[LAST][1], BLOCK), bf16),
             dma((3,)),
             dma((BLOCKS,)),
             dma((SMALLS, len(PARTS))),
@@ -612,6 +697,8 @@
             dma(()),
             dma((2,)),
             dma((2,)),
+            dma((14,)),
+            dma((BLOCKS,)),
         ],
         name="backward",
         compiler_params=pltpu.CompilerParams(

time: 140 us -> 138 us (0.986)
  Pallas kernels: 139 us -> 137 us
    pallas_call x1, Pallas kernels: 134 us -> 132 us  [backward(): pl.pallas_call(backward_kernel, out_shape=(pltpu.VMEM((TOK, D), bf16), pl...]
where the time goes in v2:
time: 138 us
  Pallas kernels  137 us (99%)
    pallas_call x1, Pallas kernels, backward(): pl.pallas_call(backward_kernel, out_shape=(pltpu.VMEM((TOK, D), bf16), pl...  132 us
    pallas_call x1, Pallas kernels, update(): pl.pallas_call(update_kernel, out_shape=(jax.ShapeDtypeStruct((1, 2, LAT,...  5.16 us

profile of v2, /device:TPU:1, one launch (start us, length us, event | category | flops | bytes accessed | tf_op | source)
XLA Modules:
  0.0 137.9 jit_solution(5582647817806292975)
XLA Ops:
  0.6 131.9 %backward.1 = (bf16[128,7168]{1,0:T(8,128)(2,1)S(1)}, bf16[2,8,256,896]{3,2,1,0:T(8,128)(2,1)S(1)}, bf16[2,2,256,256]{3,2,1,0:T(8,128)(2,1)S(1)}, f32[2,8,128]{2,1,0:T(8,128)S(1)}) custom-call(bf16[128,7168]{1,0:T(8,128)(2,1)} %bitcast.6, bf16[128,7168]{1,0:T(8,128)(2,1)} %top.1, bf16[256,7168]{1,0:T(8,128)(2,1)} %bitcast.4, bf16[256,7168]{1,0:T(8,128)(2,1)} %bitcast.5), custom_call_target="tpu_custom_call" | custom-call | tf_op jit(solution)/shard_map/backward/pallas_call | solution.py:652
  132.6 5.2 %update.1 = (bf16[1,2,256,7168]{3,2,1,0:T(8,128)(2,1)}, f32[1,2]{1,0:T(1,128)}, bf16[128,7168]{1,0:T(8,128)(2,1)}) custom-call(bf16[2,2,256,256]{3,2,1,0:T(8,128)(2,1)S(1)} %get-tuple-element.10.poly, bf16[2,8,256,896]{3,2,1,0:T(8,128)(2,1)S(1)} %get-tuple-element.11.blocks, f32[2,8,128]{2,1,0:T(8,128)S(1)} %get-tuple-element.12.norms, ...), custom_call_target="tpu_custom_call" | custom-call | tf_op jit(solution)/shard_map/update/pallas_call | solution.py:737

commit v3 on v2

--- a/solution.py
+++ b/solution.py
@@ -19,7 +19,7 @@
 SMALL = 8
 SMALLS = TOK // SMALL
 PACK = D // 2
-PARTS = ((0, 1024), (1024, 1024), (2048, 1024), (3072, 512))
+PARTS = ((0, 1280), (1280, 1280), (2560, 1024))
 READY = 3
 PIECES = ((0, 64), (64, 64), (128, 80), (208, 48))
 QUARTERS = len(PIECES)

time: 138 us -> 138 us (level)
  no operation moved by 1% of the time
where the time goes in v3:
time: 138 us
  Pallas kernels  137 us (99%)
    pallas_call x1, Pallas kernels, backward(): pl.pallas_call(backward_kernel, out_shape=(pltpu.VMEM((TOK, D), bf16), pl...  132 us
    pallas_call x1, Pallas kernels, update(): pl.pallas_call(update_kernel, out_shape=(jax.ShapeDtypeStruct((1, 2, LAT,...  5.16 us

profile of v3, /device:TPU:1, one launch (start us, length us, event | category | flops | bytes accessed | tf_op | source)
XLA Modules:
  0.0 137.5 jit_solution(15031846903856727498)
XLA Ops:
  0.6 131.6 %backward.1 = (bf16[128,7168]{1,0:T(8,128)(2,1)S(1)}, bf16[2,8,256,896]{3,2,1,0:T(8,128)(2,1)S(1)}, bf16[2,2,256,256]{3,2,1,0:T(8,128)(2,1)S(1)}, f32[2,8,128]{2,1,0:T(8,128)S(1)}) custom-call(bf16[128,7168]{1,0:T(8,128)(2,1)} %bitcast.6, bf16[128,7168]{1,0:T(8,128)(2,1)} %top.1, bf16[256,7168]{1,0:T(8,128)(2,1)} %bitcast.4, bf16[256,7168]{1,0:T(8,128)(2,1)} %bitcast.5), custom_call_target="tpu_custom_call" | custom-call | tf_op jit(solution)/shard_map/backward/pallas_call | solution.py:652
  132.2 5.2 %update.1 = (bf16[1,2,256,7168]{3,2,1,0:T(8,128)(2,1)}, f32[1,2]{1,0:T(1,128)}, bf16[128,7168]{1,0:T(8,128)(2,1)}) custom-call(bf16[2,2,256,256]{3,2,1,0:T(8,128)(2,1)S(1)} %get-tuple-element.10.poly, bf16[2,8,256,896]{3,2,1,0:T(8,128)(2,1)S(1)} %get-tuple-element.11.blocks, f32[2,8,128]{2,1,0:T(8,128)S(1)} %get-tuple-element.12.norms, ...), custom_call_target="tpu_custom_call" | custom-call | tf_op jit(solution)/shard_map/update/pallas_call | solution.py:737
